TPU v7x, 512 devices: a whole 4x8x8 slice. The times are simulated.
512 devices in a mesh: az: 128 (over z, x, y_hi), ch: 4 (over y_lo, core).
Axes of the slice: x: 4, y: 8 (y_hi: 4, y_lo: 2; y = y_hi * 2 + y_lo), z: 8, core: 2. Of those that a mesh axis runs over, the one named last changes fastest.
Arguments:
- features: bfloat16 [256, 512, 256], P(None, 'az'), may hold values from -6 to 6
- conv1_weight: bfloat16 [256, 3, 3, 256], P('ch'), may hold values from -0.125 to 0.125
- conv1_bias: float32 [256], P('ch'), may hold values from -3 to 3
- conv2_weight: bfloat16 [256, 3, 3, 256], P('ch'), may hold values from -0.125 to 0.125
- conv2_bias: float32 [256], P('ch'), may hold values from -3 to 3
- request_cell: int32 [524288], P('az'), may hold values from 0 to 1023, as said below
- corner_slot: int32 [4, 65536], P(None, 'az'), may hold values from 0 to 4095, as said below
- corner_frac: float32 [2, 65536], P(None, 'az'), may hold values from 0 to 1
- expand_weight: bfloat16 [256, 512], P('ch'), may hold values from -0.375 to 0.375
- expand_bias: float32 [512], P('ch'), may hold values from -3 to 3
Outputs:
- occupancy: bfloat16 [512, 65536], P('ch', 'az')
Inputs may be any that keep to these rules, and one draw needn't show every extreme that they name: `request_cell`: cell index a * 256 + r within the sector that the slot's block names; entries of slots that no corner_slot entry names are never read. `corner_slot`: within one tile the 2048 entries name distinct slots; at most 32 slots of one sector block are named, exactly 32 for some sector of every tile.
All inputs are finite; a program needn't handle non-finite values.
Results may differ from a plain program's by a relative error of at most 0.014.
Values may be sent and summed in bfloat16 or wider, within the bound.
A program may use at most 64 MiB of HBM per device.

v0:
```python
import jax
import jax.numpy as jnp
from jax import lax
from jax.sharding import PartitionSpec as P


def padded_2(array, sides, width):
    for axis, dim in sides:
        size, length = (lax.axis_size(axis), array.shape[dim])
        up = [(i, (i + 1) % size) for i in range(size)]
        down = [(j, i) for i, j in up]
        last = lax.slice_in_dim(array, length - width, length, axis=dim)
        first = lax.slice_in_dim(array, 0, width, axis=dim)
        before = lax.ppermute(last, axis, up)
        after = lax.ppermute(first, axis, down)
        array = jnp.concatenate([before, array, after], axis=dim)
    return array


def convolve(padded, weight, columns, ranges):
    inputs = padded.shape[0]
    ranged = jnp.pad(padded, ((0, 0), (0, 0), (1, 1)))
    running = jnp.zeros((weight.shape[0], columns * ranges), jnp.float32)
    for tap_az in range(3):
        for tap_rg in range(3):
            window = ranged[:, tap_az : tap_az + columns, tap_rg : tap_rg + ranges].reshape(
                inputs, columns * ranges
            )
            running = running + jnp.dot(
                weight[:, tap_az, tap_rg, :], window, preferred_element_type=jnp.float32
            )
    return running


def local(
    features,
    conv1_weight,
    conv1_bias,
    conv2_weight,
    conv2_bias,
    request_cell,
    corner_slot,
    corner_frac,
    expand_weight,
    expand_bias,
):
    columns = features.shape[1]
    ranges = features.shape[2]
    outputs = conv1_weight.shape[0]
    widened = padded_2(features, (("az", 1),), 1)
    hidden_one = jax.nn.relu(
        convolve(widened, conv1_weight, columns, ranges) + conv1_bias[:, None]
    ).astype(jnp.bfloat16)
    hidden_one = padded_2(hidden_one.reshape(outputs, columns, ranges), (("az", 1),), 1)
    second_sum = convolve(
        lax.all_gather(hidden_one, "ch", axis=0, tiled=True), conv2_weight, columns, ranges
    )
    hidden_two = jax.nn.relu(second_sum + conv2_bias[:, None]).astype(jnp.bfloat16)
    asked_cells = lax.all_to_all(request_cell, "az", split_axis=0, concat_axis=0, tiled=True)
    picked_cells = jnp.take(hidden_two, asked_cells, axis=1)
    arrived = lax.all_to_all(picked_cells, "az", split_axis=1, concat_axis=1, tiled=True)
    frac_range = corner_frac[0][None, :]
    frac_azim = corner_frac[1][None, :]
    weights = [
        (1.0 - frac_range) * (1.0 - frac_azim),
        frac_range * (1.0 - frac_azim),
        (1.0 - frac_range) * frac_azim,
        frac_range * frac_azim,
    ]
    resampled = jnp.zeros((outputs, corner_slot.shape[1]), jnp.float32)
    for k in range(4):
        resampled = resampled + weights[k] * jnp.take(arrived, corner_slot[k], axis=1).astype(
            jnp.float32
        )
    resampled = resampled.astype(jnp.bfloat16)
    share_rows = expand_weight.shape[1] // lax.axis_size("ch")
    partial_term = lax.dot_general(
        expand_weight, resampled, (((0,), (0,)), ((), ())), preferred_element_type=jnp.float32
    )
    summed = lax.psum(partial_term.astype(jnp.bfloat16), "ch").astype(jnp.float32)
    own_rows = lax.dynamic_slice_in_dim(summed, lax.axis_index("ch") * share_rows, share_rows, 0)
    return (own_rows + expand_bias[:, None]).astype(jnp.bfloat16)


def solution(mesh):
    return jax.shard_map(
        local,
        mesh=mesh,
        in_specs=(
            P(None, "az", None),
            P("ch", None, None, None),
            P("ch"),
            P("ch", None, None, None),
            P("ch"),
            P("az"),
            P(None, "az"),
            P(None, "az"),
            P("ch", None),
            P("ch"),
        ),
        out_specs=P("ch", "az"),
        check_vma=False,
    )
```

profile of v0, /device:TPU:1, one launch (start us, length us, event | category | flops | bytes accessed | tf_op | source)
XLA Modules:
  0.0 193.8 jit_solution(11583841178571506555)
XLA Ops:
  6.5 1.7 fusion.78
  8.3 5.0 %collective-permute-start = (bf16[256,1,256]{2,1,0:T(2,128)(2,1)S(1)}, bf16[256,1,256]{2,1,0:T(2,128)(2,1)S(1)}, u32[]{:S(2)}, u32[]{:S(2)}) collective-permute-start(bf16[256,1,256]{2,1,0:T(2,128)(2,1)S(1)} %get-tuple-element.23), channel_id=1, source_target_pairs={{0,4},{4,8},{8,12},{12,16},{16,20},{20,24},{24,28},{28,32},{32,36}... | collective-permute-start | bytes 393224 | tf_op jit(solution)/shard_map/ppermute | solution.py:14
  13.3 14.3 %collective-permute-start.1 = (bf16[256,1,256]{2,1,0:T(2,128)(2,1)S(1)}, bf16[256,1,256]{2,1,0:T(2,128)(2,1)S(1)}, u32[]{:S(2)}, u32[]{:S(2)}) collective-permute-start(bf16[256,1,256]{2,1,0:T(2,128)(2,1)S(1)} %get-tuple-element.24), channel_id=1, source_target_pairs={{4,0},{8,4},{12,8},{16,12},{20,16},{24,20},{28,24},{32,28},{36,32}... | collective-permute-start | bytes 393224 | tf_op jit(solution)/shard_map/ppermute | solution.py:15
  27.6 1.4 all_to_all.16
  29.0 8.9 %all-to-all-start = ((s32[128,32,1]{1,2,0:T(1,128)}), s32[128,32,1]{1,2,0:T(1,128)S(1)}, u32[]{:S(2)}, u32[]{:S(2)}) async-start(s32[128,32,1]{1,2,0:T(1,128)} %bitcast.2), calls=%async_computation | async-start | bytes 131072 | tf_op jit(solution)/shard_map/all_to_all | solution.py:59
  38.4 12.6 %all-to-all-done = s32[128,32,1]{1,2,0:T(1,128)S(1)} async-done(((s32[128,32,1]{1,2,0:T(1,128)}), s32[128,32,1]{1,2,0:T(1,128)S(1)}, u32[]{:S(2)}, u32[]{:S(2)}) %all-to-all-start) | async-done | bytes 16416 | tf_op jit(solution)/shard_map/all_to_all | solution.py:59
  52.5 2.4 %fusion.5 = bf16[256,6,258]{2,1,0:T(8,128)(2,1)S(1)} fusion(bf16[256,1,256]{2,1,0:T(2,128)(2,1)S(1)} %collective-permute-done.1, bf16[256,4,256]{2,1,0:T(4,128)(2,1)S(1)} %copy-done.1, bf16[256,1,256]{2,1,0:T(2,128)(2,1)S(1)} %collective-permute-done), kind=kLoop, calls=%fused_computation.12 | loop fusion | flops 4755456 | bytes 1579008 | tf_op jit(solution)/shard_map/concatenate | solution.py:16
  54.9 1.8 fusion.77
  57.1 1.2 pad_maximum_fusion
  60.5 2.2 %collective-permute-start.2 = (bf16[64,1,256]{2,0,1:T(8,128)(2,1)S(1)}, bf16[64,1,256]{2,0,1:T(8,128)(2,1)S(1)}, u32[]{:S(2)}, u32[]{:S(2)}) collective-permute-start(bf16[64,1,256]{2,0,1:T(8,128)(2,1)S(1)} %get-tuple-element.25), channel_id=1, source_target_pairs={{0,4},{4,8},{8,12},{12,16},{16,20},{20,24},{24,28},{28,32},{32,36}... | collective-permute-start | bytes 98312 | tf_op jit(solution)/shard_map/ppermute | solution.py:14
  62.7 9.4 %collective-permute-start.3 = (bf16[64,1,256]{2,0,1:T(8,128)(2,1)S(1)}, bf16[64,1,256]{2,0,1:T(8,128)(2,1)S(1)}, u32[]{:S(2)}, u32[]{:S(2)}) collective-permute-start(bf16[64,1,256]{2,0,1:T(8,128)(2,1)S(1)} %get-tuple-element.26), channel_id=1, source_target_pairs={{4,0},{8,4},{12,8},{16,12},{20,16},{24,20},{28,24},{32,28},{36,32}... | collective-permute-start | bytes 98312 | tf_op jit(solution)/shard_map/ppermute | solution.py:15
  72.2 1.0 collective-permute-done.3
  73.2 11.6 %all_gather.3 = bf16[256,6,256]{2,0,1:T(8,128)(2,1)S(1)} all-gather(bf16[64,6,256]{2,0,1:T(8,128)(2,1)S(1)} %pad_maximum_fusion.2), channel_id=1, replica_groups=mesh['az'=128,'ch'=4] {'ch'}, dimensions={0}, use_global_device_ids=true | all-gather | bytes 983040 | tf_op jit(solution)/shard_map/all_gather | solution.py:56
  88.8 12.1 %gather_fusion = bf16[4096,64]{1,0:T(8,128)(2,1)S(1)} fusion(bf16[64,1024]{0,1:T(8,128)(2,1)S(1)} %copy.29, s32[4096]{0:T(1024)S(1)} %broadcast_clamp_fusion), kind=kCustom, calls=%fused_computation.4 | custom fusion | bytes 1064960 | tf_op jit(solution)/shard_map/jit(_take)/gather | solution.py:60
  101.8 1.4 reshape.189
  103.1 12.0 %all-to-all-start.1 = ((bf16[128,2,1024]{2,1,0:T(2,128)(2,1)}), bf16[128,2,1024]{2,1,0:T(2,128)(2,1)S(1)}, u32[]{:S(2)}, u32[]{:S(2)}) async-start(bf16[128,2,1024]{2,1,0:T(2,128)(2,1)} %reshape.189), calls=%async_computation.1 | async-start | bytes 1048576 | tf_op jit(solution)/shard_map/all_to_all | solution.py:61
  115.3 19.0 %all-to-all-done.1 = bf16[128,2,1024]{2,1,0:T(2,128)(2,1)S(1)} async-done(((bf16[128,2,1024]{2,1,0:T(2,128)(2,1)}), bf16[128,2,1024]{2,1,0:T(2,128)(2,1)S(1)}, u32[]{:S(2)}, u32[]{:S(2)}) %all-to-all-start.1) | async-done | bytes 524320 | tf_op jit(solution)/shard_map/all_to_all | solution.py:61
  134.9 1.3 gather_fusion.1
  136.2 1.3 gather_fusion.2
  137.6 1.3 gather_fusion.3
  138.9 1.3 gather_fusion.4
  140.3 1.7 fusion.6
  142.0 43.2 %all-reduce.4.cloned.1.call-done = bf16[512,512]{0,1:T(8,128)(2,1)} async-done(((bf16[512,512]{0,1:T(8,128)(2,1)}), bf16[512,512]{0,1:T(8,128)(2,1)}) %all-reduce.4.cloned.1.call-update) | async-done | bytes 524304 | tf_op jit(solution)/shard_map/psum | solution.py:80
  185.3 0.9 add_convert_fusion
  (77 shorter events, 10.5 us)
Async XLA Ops:
  6.5 133.8 %copy-start = (bf16[64,512]{1,0:T(8,128)(2,1)S(1)}, bf16[64,512]{1,0:T(8,128)(2,1)}, u32[]{:S(2)}) copy-start(bf16[64,512]{1,0:T(8,128)(2,1)} %param.20) | copy-start | bytes 196612
  6.5 31.4 %copy-start.1 = (bf16[256,4,256]{2,1,0:T(4,128)(2,1)S(1)}, bf16[256,4,256]{2,1,0:T(4,128)(2,1)}, u32[]{:S(2)}) copy-start(bf16[256,4,256]{2,1,0:T(4,128)(2,1)} %param.12) | copy-start | bytes 1572868
  6.5 31.5 %copy-start.4 = (s32[4,512]{1,0:T(4,128)S(1)}, s32[4,512]{1,0:T(4,128)}, u32[]{:S(2)}) copy-start(s32[4,512]{1,0:T(4,128)} %param.18) | copy-start | bytes 24580
  6.5 31.6 %copy-start.3 = (bf16[64,3,3,256]{3,0,2,1:T(8,128)(2,1)S(1)}, bf16[64,3,3,256]{3,0,2,1:T(8,128)(2,1)}, u32[]{:S(2)}) copy-start(bf16[64,3,3,256]{3,0,2,1:T(8,128)(2,1)} %param.13) | copy-start | bytes 884740
  8.3 44.2 %collective-permute-start = (bf16[256,1,256]{2,1,0:T(2,128)(2,1)S(1)}, bf16[256,1,256]{2,1,0:T(2,128)(2,1)S(1)}, u32[]{:S(2)}, u32[]{:S(2)}) collective-permute-start(bf16[256,1,256]{2,1,0:T(2,128)(2,1)S(1)} %get-tuple-element.23), channel_id=1, source_target_pairs={{0,4},{4,8},{8,12},{12,16},{16,20},{20,24},{24,28},{28,32},{32,36}... | collective-permute-start | bytes 393224 | tf_op jit(solution)/shard_map/ppermute | solution.py:14
  13.3 39.2 %collective-permute-start.1 = (bf16[256,1,256]{2,1,0:T(2,128)(2,1)S(1)}, bf16[256,1,256]{2,1,0:T(2,128)(2,1)S(1)}, u32[]{:S(2)}, u32[]{:S(2)}) collective-permute-start(bf16[256,1,256]{2,1,0:T(2,128)(2,1)S(1)} %get-tuple-element.24), channel_id=1, source_target_pairs={{4,0},{8,4},{12,8},{16,12},{20,16},{24,20},{28,24},{32,28},{36,32}... | collective-permute-start | bytes 393224 | tf_op jit(solution)/shard_map/ppermute | solution.py:15
  29.0 22.0 %all-to-all-start = ((s32[128,32,1]{1,2,0:T(1,128)}), s32[128,32,1]{1,2,0:T(1,128)S(1)}, u32[]{:S(2)}, u32[]{:S(2)}) async-start(s32[128,32,1]{1,2,0:T(1,128)} %bitcast.2), calls=%async_computation | async-start | bytes 131072 | tf_op jit(solution)/shard_map/all_to_all | solution.py:59
  59.6 0.7 copy-start.6
  60.5 11.6 %collective-permute-start.2 = (bf16[64,1,256]{2,0,1:T(8,128)(2,1)S(1)}, bf16[64,1,256]{2,0,1:T(8,128)(2,1)S(1)}, u32[]{:S(2)}, u32[]{:S(2)}) collective-permute-start(bf16[64,1,256]{2,0,1:T(8,128)(2,1)S(1)} %get-tuple-element.25), channel_id=1, source_target_pairs={{0,4},{4,8},{8,12},{12,16},{16,20},{20,24},{24,28},{28,32},{32,36}... | collective-permute-start | bytes 98312 | tf_op jit(solution)/shard_map/ppermute | solution.py:14
  62.7 10.4 %collective-permute-start.3 = (bf16[64,1,256]{2,0,1:T(8,128)(2,1)S(1)}, bf16[64,1,256]{2,0,1:T(8,128)(2,1)S(1)}, u32[]{:S(2)}, u32[]{:S(2)}) collective-permute-start(bf16[64,1,256]{2,0,1:T(8,128)(2,1)S(1)} %get-tuple-element.26), channel_id=1, source_target_pairs={{4,0},{8,4},{12,8},{16,12},{20,16},{24,20},{28,24},{32,28},{36,32}... | collective-permute-start | bytes 98312 | tf_op jit(solution)/shard_map/ppermute | solution.py:15
  85.0 1.0 copy-start.2
  87.4 0.9 copy-start.7
  101.7 13.5 %copy-start.5 = (f32[2,512]{1,0:T(2,128)S(1)}, f32[2,512]{1,0:T(2,128)}, u32[]{:S(2)}) copy-start(f32[2,512]{1,0:T(2,128)} %param.19) | copy-start | bytes 12292
  103.1 31.1 %all-to-all-start.1 = ((bf16[128,2,1024]{2,1,0:T(2,128)(2,1)}), bf16[128,2,1024]{2,1,0:T(2,128)(2,1)S(1)}, u32[]{:S(2)}, u32[]{:S(2)}) async-start(bf16[128,2,1024]{2,1,0:T(2,128)(2,1)} %reshape.189), calls=%async_computation.1 | async-start | bytes 1048576 | tf_op jit(solution)/shard_map/all_to_all | solution.py:61
  115.1 70.1 %all-reduce.4.cloned.1.call-start = ((), (), s32[]{:S(2)}) async-start(), calls=%async_computation.2 | async-start | bytes 1048576 | tf_op jit(solution)/shard_map/psum | solution.py:80
  137.6 47.7 %copy-start.8 = (f32[128]{0:T(128)S(1)}, f32[128]{0:T(128)}, u32[]{:S(2)}) copy-start(f32[128]{0:T(128)} %param.21) | copy-start | bytes 1540
Sparse Core Ops, SparseCore 0:
  142.1 43.0 all-reduce.3
where the time goes:
time: 194 us
  waiting for transfers between devices  75.9 us (39%)
  starting transfers between devices  51.8 us (27%)
  local copies, waits for them, and re-layouts  28.1 us (14%)
  between operations  14 us (7%)
  blocking collectives  11.6 us (6%)
  other arithmetic  6.25 us (3%)
  matrix products  6.14 us (3%)
    psum x1, waiting for transfers between devices, local(): lax.psum(partial_term.astype(jnp.bfloat16), 'ch').astype(jnp.float32)  43.2 us
    ppermute x2, starting transfers between devices, padded_2(): after = lax.ppermute(first, axis, down)  23.7 us
    all_to_all x1, waiting for transfers between devices, local(): lax.all_to_all(picked_cells, 'az', split_axis=1, concat_axis=1, tiled=True)  19 us
    all_to_all x1, waiting for transfers between devices, local(): lax.all_to_all(request_cell, 'az', split_axis=0, concat_axis=0, tiled=True)  12.6 us
    gather x1, local copies, waits for them, and re-layouts, local(): picked_cells = jnp.take(hidden_two, asked_cells, axis=1)  12.1 us
    all_to_all x1, starting transfers between devices, local(): lax.all_to_all(picked_cells, 'az', split_axis=1, concat_axis=1, tiled=True)  12 us
    all_gather x1, blocking collectives, local(): lax.all_gather(hidden_one, 'ch', axis=0, tiled=True)  11.6 us
    all_to_all x1, starting transfers between devices, local(): lax.all_to_all(request_cell, 'az', split_axis=0, concat_axis=0, tiled=True)  8.91 us
  transfers between devices with their start and end apart: 7, of which 4 were waited for; matrix products, arithmetic and copies ran while one was open for 1% of the time, Pallas kernels for 0%

commit v1 on v0

--- a/solution.py
+++ b/solution.py
@@ -77,7 +77,9 @@
     partial_term = lax.dot_general(
         expand_weight, resampled, (((0,), (0,)), ((), ())), preferred_element_type=jnp.float32
     )
-    summed = lax.psum(partial_term.astype(jnp.bfloat16), "ch").astype(jnp.float32)
+    summed = jnp.sum(lax.all_gather(partial_term.astype(jnp.bfloat16), "ch"), axis=0).astype(
+        jnp.float32
+    )
     own_rows = lax.dynamic_slice_in_dim(summed, lax.axis_index("ch") * share_rows, share_rows, 0)
     return (own_rows + expand_bias[:, None]).astype(jnp.bfloat16)
 

time: 194 us -> 186 us (0.959)
  waiting for transfers between devices: 75.9 us -> 61.2 us
  local copies, waits for them, and re-layouts: 28.1 us -> 32.5 us
    psum x1 -> x0, waiting for transfers between devices: 43.2 us -> none  [local(): lax.psum(partial_term.astype(jnp.bfloat16), 'ch').astype(jnp.float32)]
    all_gather x0 -> x1, waiting for transfers between devices: none -> 29.6 us  [local(): lax.all_gather(partial_term.astype(jnp.bfloat16), 'ch')]
    all_gather x0 -> x1, local copies, waits for them, and re-layouts: none -> 3.31 us  [local(): lax.all_gather(partial_term.astype(jnp.bfloat16), 'ch')]
    reduce_sum x0 -> x1, other arithmetic: none -> 2.8 us  [local(): jnp.sum(lax.all_gather(partial_term.astype(jnp.bfloat16), 'ch'), axis=0)]
  transfers between devices with their start and end apart: 7 -> 7, of which waited for: 4 -> 4; matrix products, arithmetic and copies ran while one was open for 1% -> 2% of each run, Pallas kernels for 0% -> 0%
where the time goes in v1:
time: 186 us; the launch traced here: 185 us
  waiting for transfers between devices  61.2 us (33%)
  starting transfers between devices  51.8 us (28%)
  local copies, waits for them, and re-layouts  32.5 us (17%)
  between operations  14 us (8%)
  blocking collectives  11.6 us (6%)
  other arithmetic  8.15 us (4%)
  matrix products  6.15 us (3%)
    all_gather x1, waiting for transfers between devices, local(): lax.all_gather(partial_term.astype(jnp.bfloat16), 'ch')  29.6 us
    ppermute x2, starting transfers between devices, padded_2(): after = lax.ppermute(first, axis, down)  23.7 us
    all_to_all x1, waiting for transfers between devices, local(): lax.all_to_all(picked_cells, 'az', split_axis=1, concat_axis=1, tiled=True)  19 us
    gather x1, local copies, waits for them, and re-layouts, local(): picked_cells = jnp.take(hidden_two, asked_cells, axis=1)  12.1 us
    all_to_all x1, starting transfers between devices, local(): lax.all_to_all(picked_cells, 'az', split_axis=1, concat_axis=1, tiled=True)  12 us
    all_to_all x1, waiting for transfers between devices, local(): lax.all_to_all(request_cell, 'az', split_axis=0, concat_axis=0, tiled=True)  11.6 us
    all_gather x1, blocking collectives, local(): lax.all_gather(hidden_one, 'ch', axis=0, tiled=True)  11.6 us
    all_to_all x1, starting transfers between devices, local(): lax.all_to_all(request_cell, 'az', split_axis=0, concat_axis=0, tiled=True)  8.91 us
  transfers between devices with their start and end apart: 7, of which 4 were waited for; matrix products, arithmetic and copies ran while one was open for 2% of the time, Pallas kernels for 0%

profile of v1, /device:TPU:1, one launch (start us, length us, event | category | flops | bytes accessed | tf_op | source)
XLA Modules:
  0.0 185.5 jit_solution(11710892635472603982)
XLA Ops:
  6.5 1.8 fusion.78
  8.3 5.0 %collective-permute-start = (bf16[256,1,256]{2,1,0:T(2,128)(2,1)S(1)}, bf16[256,1,256]{2,1,0:T(2,128)(2,1)S(1)}, u32[]{:S(2)}, u32[]{:S(2)}) collective-permute-start(bf16[256,1,256]{2,1,0:T(2,128)(2,1)S(1)} %get-tuple-element.23), channel_id=1, source_target_pairs={{0,4},{4,8},{8,12},{12,16},{16,20},{20,24},{24,28},{28,32},{32,36}... | collective-permute-start | bytes 393224 | tf_op jit(solution)/shard_map/ppermute | solution.py:14
  13.4 14.3 %collective-permute-start.1 = (bf16[256,1,256]{2,1,0:T(2,128)(2,1)S(1)}, bf16[256,1,256]{2,1,0:T(2,128)(2,1)S(1)}, u32[]{:S(2)}, u32[]{:S(2)}) collective-permute-start(bf16[256,1,256]{2,1,0:T(2,128)(2,1)S(1)} %get-tuple-element.24), channel_id=1, source_target_pairs={{4,0},{8,4},{12,8},{16,12},{20,16},{24,20},{28,24},{32,28},{36,32}... | collective-permute-start | bytes 393224 | tf_op jit(solution)/shard_map/ppermute | solution.py:15
  27.6 1.4 all_to_all.16
  29.1 8.9 %all-to-all-start = ((s32[128,32,1]{1,2,0:T(1,128)}), s32[128,32,1]{1,2,0:T(1,128)S(1)}, u32[]{:S(2)}, u32[]{:S(2)}) async-start(s32[128,32,1]{1,2,0:T(1,128)} %bitcast.2), calls=%async_computation | async-start | bytes 131072 | tf_op jit(solution)/shard_map/all_to_all | solution.py:59
  39.4 11.6 %all-to-all-done = s32[128,32,1]{1,2,0:T(1,128)S(1)} async-done(((s32[128,32,1]{1,2,0:T(1,128)}), s32[128,32,1]{1,2,0:T(1,128)S(1)}, u32[]{:S(2)}, u32[]{:S(2)}) %all-to-all-start) | async-done | bytes 16416 | tf_op jit(solution)/shard_map/all_to_all | solution.py:59
  52.5 2.4 %fusion.5 = bf16[256,6,258]{2,1,0:T(8,128)(2,1)S(1)} fusion(bf16[256,1,256]{2,1,0:T(2,128)(2,1)S(1)} %collective-permute-done.1, bf16[256,4,256]{2,1,0:T(4,128)(2,1)S(1)} %copy-done.1, bf16[256,1,256]{2,1,0:T(2,128)(2,1)S(1)} %collective-permute-done), kind=kLoop, calls=%fused_computation.12 | loop fusion | flops 4755456 | bytes 1579008 | tf_op jit(solution)/shard_map/concatenate | solution.py:16
  54.9 1.8 fusion.77
  57.1 1.2 pad_maximum_fusion
  60.5 2.2 %collective-permute-start.2 = (bf16[64,1,256]{2,0,1:T(8,128)(2,1)S(1)}, bf16[64,1,256]{2,0,1:T(8,128)(2,1)S(1)}, u32[]{:S(2)}, u32[]{:S(2)}) collective-permute-start(bf16[64,1,256]{2,0,1:T(8,128)(2,1)S(1)} %get-tuple-element.25), channel_id=1, source_target_pairs={{0,4},{4,8},{8,12},{12,16},{16,20},{20,24},{24,28},{28,32},{32,36}... | collective-permute-start | bytes 98312 | tf_op jit(solution)/shard_map/ppermute | solution.py:14
  62.8 9.4 %collective-permute-start.3 = (bf16[64,1,256]{2,0,1:T(8,128)(2,1)S(1)}, bf16[64,1,256]{2,0,1:T(8,128)(2,1)S(1)}, u32[]{:S(2)}, u32[]{:S(2)}) collective-permute-start(bf16[64,1,256]{2,0,1:T(8,128)(2,1)S(1)} %get-tuple-element.26), channel_id=1, source_target_pairs={{4,0},{8,4},{12,8},{16,12},{20,16},{24,20},{28,24},{32,28},{36,32}... | collective-permute-start | bytes 98312 | tf_op jit(solution)/shard_map/ppermute | solution.py:15
  73.2 11.6 %all_gather.9 = bf16[256,6,256]{2,0,1:T(8,128)(2,1)S(1)} all-gather(bf16[64,6,256]{2,0,1:T(8,128)(2,1)S(1)} %pad_maximum_fusion.2), channel_id=1, replica_groups=mesh['az'=128,'ch'=4] {'ch'}, dimensions={0}, use_global_device_ids=true | all-gather | bytes 983040 | tf_op jit(solution)/shard_map/all_gather | solution.py:56
  88.8 12.1 %gather_fusion = bf16[4096,64]{1,0:T(8,128)(2,1)S(1)} fusion(bf16[64,1024]{0,1:T(8,128)(2,1)S(1)} %copy.27, s32[4096]{0:T(1024)S(1)} %broadcast_clamp_fusion), kind=kCustom, calls=%fused_computation.4 | custom fusion | bytes 1064960 | tf_op jit(solution)/shard_map/jit(_take)/gather | solution.py:60
  101.8 1.4 reshape.190
  103.2 12.0 %all-to-all-start.1 = ((bf16[128,2,1024]{2,1,0:T(2,128)(2,1)}), bf16[128,2,1024]{2,1,0:T(2,128)(2,1)S(1)}, u32[]{:S(2)}, u32[]{:S(2)}) async-start(bf16[128,2,1024]{2,1,0:T(2,128)(2,1)} %reshape.190), calls=%async_computation.1 | async-start | bytes 1048576 | tf_op jit(solution)/shard_map/all_to_all | solution.py:61
  115.3 19.0 %all-to-all-done.1 = bf16[128,2,1024]{2,1,0:T(2,128)(2,1)S(1)} async-done(((bf16[128,2,1024]{2,1,0:T(2,128)(2,1)}), bf16[128,2,1024]{2,1,0:T(2,128)(2,1)S(1)}, u32[]{:S(2)}, u32[]{:S(2)}) %all-to-all-start.1) | async-done | bytes 524320 | tf_op jit(solution)/shard_map/all_to_all | solution.py:61
  134.9 1.3 gather_fusion.1
  136.3 1.3 gather_fusion.2
  137.6 1.3 gather_fusion.3
  139.0 1.3 gather_fusion.4
  140.3 1.7 fusion.6
  142.1 29.6 %all-gather.3.cloned.1.call-done = bf16[2048,512]{0,1:T(8,128)(2,1)} async-done(((bf16[512,512]{0,1:T(8,128)(2,1)}), bf16[2048,512]{0,1:T(8,128)(2,1)}) %all-gather.3.cloned.1.call-update) | async-done | bytes 2097168 | tf_op jit(solution)/shard_map/all_gather | solution.py:80
  171.7 3.3 %reshape.168 = bf16[4,512,512]{1,0,2:T(4,128)(2,1)S(1)} reshape(bf16[2048,512]{0,1:T(8,128)(2,1)} %all-gather.3.cloned.1.call-done) | data formatting | bytes 4194304 | tf_op jit(solution)/shard_map/all_gather | solution.py:80
  175.0 2.8 %reduce_sum.12 = bf16[512,512]{0,1:T(8,128)(2,1)S(1)} reduce(bf16[4,512,512]{1,0,2:T(4,128)(2,1)S(1)} %reshape.168, bf16[]{:T(256)} %constant.26.clone.1), dimensions={0}, to_apply=%region_0.2 | reduce | flops 786432 | bytes 2621442 | tf_op jit(solution)/shard_map/reduce_sum | solution.py:80
  (79 shorter events, 12.6 us)
Async XLA Ops:
  6.5 133.8 %copy-start = (bf16[64,512]{1,0:T(8,128)(2,1)S(1)}, bf16[64,512]{1,0:T(8,128)(2,1)}, u32[]{:S(2)}) copy-start(bf16[64,512]{1,0:T(8,128)(2,1)} %param.20) | copy-start | bytes 196612
  6.5 46.0 %copy-start.1 = (bf16[256,4,256]{2,1,0:T(4,128)(2,1)S(1)}, bf16[256,4,256]{2,1,0:T(4,128)(2,1)}, u32[]{:S(2)}) copy-start(bf16[256,4,256]{2,1,0:T(4,128)(2,1)} %param.12) | copy-start | bytes 1572868
  6.5 32.6 %copy-start.4 = (s32[4,512]{1,0:T(4,128)S(1)}, s32[4,512]{1,0:T(4,128)}, u32[]{:S(2)}) copy-start(s32[4,512]{1,0:T(4,128)} %param.18) | copy-start | bytes 24580
  6.5 32.6 %copy-start.3 = (bf16[64,3,3,256]{3,0,2,1:T(8,128)(2,1)S(1)}, bf16[64,3,3,256]{3,0,2,1:T(8,128)(2,1)}, u32[]{:S(2)}) copy-start(bf16[64,3,3,256]{3,0,2,1:T(8,128)(2,1)} %param.13) | copy-start | bytes 884740
  8.3 44.2 %collective-permute-start = (bf16[256,1,256]{2,1,0:T(2,128)(2,1)S(1)}, bf16[256,1,256]{2,1,0:T(2,128)(2,1)S(1)}, u32[]{:S(2)}, u32[]{:S(2)}) collective-permute-start(bf16[256,1,256]{2,1,0:T(2,128)(2,1)S(1)} %get-tuple-element.23), channel_id=1, source_target_pairs={{0,4},{4,8},{8,12},{12,16},{16,20},{20,24},{24,28},{28,32},{32,36}... | collective-permute-start | bytes 393224 | tf_op jit(solution)/shard_map/ppermute | solution.py:14
  13.4 39.2 %collective-permute-start.1 = (bf16[256,1,256]{2,1,0:T(2,128)(2,1)S(1)}, bf16[256,1,256]{2,1,0:T(2,128)(2,1)S(1)}, u32[]{:S(2)}, u32[]{:S(2)}) collective-permute-start(bf16[256,1,256]{2,1,0:T(2,128)(2,1)S(1)} %get-tuple-element.24), channel_id=1, source_target_pairs={{4,0},{8,4},{12,8},{16,12},{20,16},{24,20},{28,24},{32,28},{36,32}... | collective-permute-start | bytes 393224 | tf_op jit(solution)/shard_map/ppermute | solution.py:15
  29.1 22.0 %all-to-all-start = ((s32[128,32,1]{1,2,0:T(1,128)}), s32[128,32,1]{1,2,0:T(1,128)S(1)}, u32[]{:S(2)}, u32[]{:S(2)}) async-start(s32[128,32,1]{1,2,0:T(1,128)} %bitcast.2), calls=%async_computation | async-start | bytes 131072 | tf_op jit(solution)/shard_map/all_to_all | solution.py:59
  59.4 0.9 copy-start.6
  60.5 11.6 %collective-permute-start.2 = (bf16[64,1,256]{2,0,1:T(8,128)(2,1)S(1)}, bf16[64,1,256]{2,0,1:T(8,128)(2,1)S(1)}, u32[]{:S(2)}, u32[]{:S(2)}) collective-permute-start(bf16[64,1,256]{2,0,1:T(8,128)(2,1)S(1)} %get-tuple-element.25), channel_id=1, source_target_pairs={{0,4},{4,8},{8,12},{12,16},{16,20},{20,24},{24,28},{28,32},{32,36}... | collective-permute-start | bytes 98312 | tf_op jit(solution)/shard_map/ppermute | solution.py:14
  62.8 10.4 %collective-permute-start.3 = (bf16[64,1,256]{2,0,1:T(8,128)(2,1)S(1)}, bf16[64,1,256]{2,0,1:T(8,128)(2,1)S(1)}, u32[]{:S(2)}, u32[]{:S(2)}) collective-permute-start(bf16[64,1,256]{2,0,1:T(8,128)(2,1)S(1)} %get-tuple-element.26), channel_id=1, source_target_pairs={{4,0},{8,4},{12,8},{16,12},{20,16},{24,20},{28,24},{32,28},{36,32}... | collective-permute-start | bytes 98312 | tf_op jit(solution)/shard_map/ppermute | solution.py:15
  85.1 1.0 copy-start.2
  87.2 1.2 copy-start.7
  101.0 14.3 %copy-start.5 = (f32[2,512]{1,0:T(2,128)S(1)}, f32[2,512]{1,0:T(2,128)}, u32[]{:S(2)}) copy-start(f32[2,512]{1,0:T(2,128)} %param.19) | copy-start | bytes 12292
  103.2 31.1 %all-to-all-start.1 = ((bf16[128,2,1024]{2,1,0:T(2,128)(2,1)}), bf16[128,2,1024]{2,1,0:T(2,128)(2,1)S(1)}, u32[]{:S(2)}, u32[]{:S(2)}) async-start(bf16[128,2,1024]{2,1,0:T(2,128)(2,1)} %reshape.190), calls=%async_computation.1 | async-start | bytes 1048576 | tf_op jit(solution)/shard_map/all_to_all | solution.py:61
  115.2 56.5 %all-gather.3.cloned.1.call-start = ((), (), s32[]{:S(2)}) async-start(), calls=%async_computation.2 | async-start | bytes 2621440 | tf_op jit(solution)/shard_map/all_gather | solution.py:80
  175.0 2.8 %copy-start.8 = (f32[128]{0:T(128)S(1)}, f32[128]{0:T(128)}, u32[]{:S(2)}) copy-start(f32[128]{0:T(128)} %param.21) | copy-start | bytes 1540
Sparse Core Ops, SparseCore 0:
  142.2 29.4 all-gather.2
